TPU v7x, 128 devices: a whole 4x4x4 slice. The times are simulated.
128 devices in a mesh: cell: 16 (over z, x), level: 4 (over y), rep: 2 (over core).
Axes of the slice: x: 4, y: 4, z: 4, core: 2. Of those that a mesh axis runs over, the one named last changes fastest.
Arguments:
- resident_pos: float32 [2, 32, 128, 2048], P(None, 'rep', 'level', 'cell'), may hold values from -0.5 to 0.5
- resident_strength: float32 [32, 128, 2048], P('rep', 'level', 'cell'), may hold values from -0.51 to 0.51
- mover_pos: float32 [2, 2, 4, 65536], P(None, 'rep', 'level', 'cell'), may hold values from -0.5 to 0.5
- mover_strength: float32 [2, 4, 65536], P('rep', 'level', 'cell'), may hold values from -0.51 to 0.51
- mover_owner: int32 [2, 4, 65536], P('rep', 'level', 'cell'), may hold values from 0 to 15, as said below
- mover_leaf: int32 [2, 4, 65536], P('rep', 'level', 'cell'), may hold values from 0 to 4095, as said below
- mover_slot: int32 [2, 4, 65536], P('rep', 'level', 'cell'), may hold values from 0 to 15
Outputs:
- velocity: float32 [2, 32, 128, 2048], P(None, 'rep', 'level', 'cell')
Inputs may be any that keep to these rules, and one draw needn't show every extreme that they name: `mover_owner`: for one rep and level index, the 4096 movers of one device name one owner at most 1024 times, and one owner is named exactly 1024 times by every device. `mover_leaf`: leaf key y * 128 + x inside the owner's domain; for one rep and level index no (owner, leaf, slot) triple appears twice.
All inputs are finite; a program needn't handle non-finite values.
Results may differ from a plain program's by a relative error of at most 0.0003.
Values sent between devices are 32-bit elements; how exact they have to be, the bound alone decides.
No kernel may reach another device: no remote copies, remote signals or barrier semaphores. Data moves between devices by JAX's collectives and lax.ppermute only.
A program may use at most 192 MiB of HBM per device.

v0:
```python
import math
import jax
import jax.numpy as jnp
import numpy as np
from jax import lax
from jax.sharding import PartitionSpec as P

ORDER = 10
HALO_LEVELS = 4
CAP = 1024
precise = lax.Precision.HIGHEST
blob_square = 0.09


def with_halo(shard, sides, width):
    for axis, dim in sides:
        devices, length = (lax.axis_size(axis), shard.shape[dim])
        up = [(i, (i + 1) % devices) for i in range(devices - 1)]
        down = [(j, i) for i, j in up]
        last = lax.slice_in_dim(shard, length - width, length, axis=dim)
        first = lax.slice_in_dim(shard, 0, width, axis=dim)
        before = lax.ppermute(last, axis, up)
        after = lax.ppermute(first, axis, down)
        shard = jnp.concatenate([before, shard, after], axis=dim)
    return shard


def real_form(matrix):
    top_rows = np.concatenate([matrix.real, -matrix.imag], axis=1)
    low_rows = np.concatenate([matrix.imag, matrix.real], axis=1)
    return np.concatenate([top_rows, low_rows], axis=0)


def child_offset(parity_x, parity_y):
    return complex((parity_x - 0.5) / 2.0, (parity_y - 0.5) / 2.0)


def upward_table(parity_x, parity_y):
    offset = child_offset(parity_x, parity_y)
    matrix = np.zeros((ORDER, ORDER), complex)
    for k in range(ORDER):
        for m in range(k + 1):
            matrix[k, m] = math.comb(k, m) * 0.5**m * offset ** (k - m)
    return real_form(matrix)


def downward_table(parity_x, parity_y):
    offset = child_offset(parity_x, parity_y)
    matrix = np.zeros((ORDER, ORDER), complex)
    for m in range(ORDER):
        for l in range(m, ORDER):
            matrix[m, l] = 0.5 ** (m + 1) * math.comb(l, m) * offset ** (l - m)
    return real_form(matrix)


def far_table(step_x, step_y):
    distance = complex(step_x, step_y)
    matrix = np.zeros((ORDER, ORDER), complex)
    for l in range(ORDER):
        for k in range(ORDER):
            matrix[l, k] = (-1) ** (k + 1) * math.comb(k + l, l) * distance ** (-(k + l + 1))
    return real_form(matrix)


def apply_matrix(matrix, level_field):
    return jnp.einsum(
        "ij,jyx->iyx", jnp.asarray(matrix, dtype=jnp.float32), level_field, precision=precise
    )


def upward(level_field):
    summed = None
    for parity_y in (0, 1):
        for parity_x in (0, 1):
            product = apply_matrix(
                upward_table(parity_x, parity_y), level_field[:, parity_y::2, parity_x::2]
            )
            summed = product if summed is None else summed + product
    return summed


def downward(parent):
    channels, cells_y, cells_x = parent.shape
    pieces = jnp.stack(
        [
            jnp.stack(
                [apply_matrix(downward_table(parity_x, parity_y), parent) for parity_x in (0, 1)]
            )
            for parity_y in (0, 1)
        ]
    )
    return pieces.transpose(2, 3, 0, 4, 1).reshape(channels, 2 * cells_y, 2 * cells_x)


def grouped_far(padded, margin_cells, cells_y, cells_x):
    classes = []
    for parity_y in (0, 1):
        row_parts = []
        for parity_x in (0, 1):
            pieces = []
            blocks = []
            for step_y in range(-2 - parity_y, 4 - parity_y):
                for step_x in range(-2 - parity_x, 4 - parity_x):
                    if max(abs(step_x), abs(step_y)) <= 1:
                        continue
                    first_y = margin_cells + parity_y + step_y
                    first_x = margin_cells + parity_x + step_x
                    pieces.append(
                        padded[:, first_y : first_y + cells_y : 2, first_x : first_x + cells_x : 2]
                    )
                    blocks.append(far_table(step_x, step_y))
            row_parts.append(
                apply_matrix(np.concatenate(blocks, axis=1), jnp.concatenate(pieces, axis=0))
            )
        classes.append(jnp.stack(row_parts))
    joined = jnp.stack(classes)
    return joined.transpose(2, 3, 0, 4, 1).reshape(joined.shape[2], cells_y, cells_x)


def top_far(level_field):
    channels, cells_y, cells_x = level_field.shape
    reach_y = cells_y - 1
    reach_x = cells_x - 1
    padded = jnp.pad(level_field, ((0, 0), (reach_y, reach_y), (reach_x, reach_x)))
    summed = jnp.zeros(level_field.shape, jnp.float32)
    for step_y in range(-reach_y, reach_y + 1):
        for step_x in range(-reach_x, reach_x + 1):
            if max(abs(step_x), abs(step_y)) <= 1:
                continue
            source = padded[
                :,
                reach_y + step_y : reach_y + step_y + cells_y,
                reach_x + step_x : reach_x + step_x + cells_x,
            ]
            summed = summed + apply_matrix(far_table(step_x, step_y), source)
    return summed


def moments(pos_x, pos_y, strength):
    real_power = jnp.ones_like(pos_x)
    imag_power = jnp.zeros_like(pos_x)
    real_rows = []
    imag_rows = []
    for k in range(ORDER):
        real_rows.append(jnp.sum(strength * real_power, axis=0))
        imag_rows.append(jnp.sum(strength * imag_power, axis=0))
        real_power, imag_power = (
            real_power * pos_x - imag_power * pos_y,
            real_power * pos_y + imag_power * pos_x,
        )
    return jnp.stack(real_rows + imag_rows)


def evaluate(local_field, pos_x, pos_y):
    real_acc = jnp.broadcast_to(local_field[ORDER - 1], pos_x.shape)
    imag_acc = jnp.broadcast_to(local_field[2 * ORDER - 1], pos_x.shape)
    for l in range(ORDER - 2, -1, -1):
        real_acc, imag_acc = (
            real_acc * pos_x - imag_acc * pos_y + local_field[l],
            real_acc * pos_y + imag_acc * pos_x + local_field[ORDER + l],
        )
    return (real_acc, imag_acc)


def framing(level_field):
    return with_halo(level_field, (("cell", 2), ("level", 1)), 3)


def local(
    resident_pos, resident_strength, mover_pos, mover_strength, mover_owner, mover_leaf, mover_slot
):
    cell_count = lax.axis_size("cell")
    level_count = lax.axis_size("level")
    half_slots, cells_y, cells_x = resident_strength.shape
    leaves = cells_y * cells_x
    owner_cell = mover_owner.reshape(-1)
    address = mover_slot.reshape(-1) * leaves + mover_leaf.reshape(-1)
    peer_ids = jnp.arange(cell_count, dtype=jnp.int32)
    onehot = (owner_cell[:, None] == peer_ids[None, :]).astype(jnp.int32)
    rank_in_owner = jnp.sum(jnp.cumsum(onehot, axis=0) * onehot, axis=1) - 1
    values = jnp.concatenate([mover_pos.reshape(2, -1), mover_strength.reshape(1, -1)])
    outgoing = (
        jnp.zeros((3, cell_count, CAP), jnp.float32).at[:, owner_cell, rank_in_owner].set(values)
    )
    addresses = (
        jnp.full((1, cell_count, CAP), half_slots * leaves, jnp.int32)
        .at[0, owner_cell, rank_in_owner]
        .set(address)
    )
    arrived, arrived_at = (
        lax.all_to_all(outgoing, "cell", split_axis=1, concat_axis=1, tiled=True),
        lax.all_to_all(addresses, "cell", split_axis=1, concat_axis=1, tiled=True),
    )
    resident = jnp.concatenate([resident_pos.reshape(2, -1), resident_strength.reshape(1, -1)])
    settled = resident.at[:, arrived_at.reshape(-1)].set(arrived.reshape(3, -1), mode="drop")
    particles = settled.reshape(3, half_slots, cells_y, cells_x)
    whole = lax.all_gather(particles, "rep", axis=1, tiled=True)
    framed = with_halo(whole, (("cell", 3), ("level", 2)), 1)
    whole_inner = framed[:, :, 1:-1, 1:-1]
    level_zero = moments(whole_inner[0], whole_inner[1], whole_inner[2])
    owned = [level_zero]
    for k in range(HALO_LEVELS):
        owned.append(upward(owned[-1]))
    framed_levels = [framing(owned[k]) for k in range(HALO_LEVELS)]
    coarse_own = owned[HALO_LEVELS]
    channels, coarse_y, coarse_x = coarse_own.shape
    collected = lax.all_gather(coarse_own[None], ("cell", "level"), axis=0, tiled=True)
    coarse_grid = collected.reshape(cell_count, level_count, channels, coarse_y, coarse_x)
    coarse_grid = coarse_grid.transpose(2, 1, 3, 0, 4).reshape(
        channels, level_count * coarse_y, cell_count * coarse_x
    )
    coarse_fields = [coarse_grid]
    top_level = min(cell_count * cells_x, level_count * cells_y).bit_length() - 1
    for k in range(HALO_LEVELS + 1, top_level + 1):
        coarse_fields.append(upward(coarse_fields[-1]))
    local_field = top_far(coarse_fields[-1])
    for index in range(len(coarse_fields) - 2, -1, -1):
        level_field = coarse_fields[index]
        padded = jnp.pad(level_field, ((0, 0), (3, 3), (3, 3)))
        local_field = grouped_far(padded, 3, level_field.shape[1], level_field.shape[2]) + downward(
            local_field
        )
    local_field = lax.dynamic_slice(
        local_field,
        (0, lax.axis_index("level") * coarse_y, lax.axis_index("cell") * coarse_x),
        (channels, coarse_y, coarse_x),
    )
    for k in range(HALO_LEVELS - 1, -1, -1):
        level_field = owned[k]
        local_field = grouped_far(
            framed_levels[k], 3, level_field.shape[1], level_field.shape[2]
        ) + downward(local_field)
    far_real, far_imag = evaluate(local_field, particles[0], particles[1])
    slot_count = framed.shape[1]
    slot_base = lax.axis_index("rep") * half_slots
    target_slots = slot_base + jnp.arange(half_slots, dtype=jnp.int32)
    keep_mask = (target_slots[:, None] != jnp.arange(slot_count, dtype=jnp.int32)[None, :]).astype(
        jnp.float32
    )[:, :, None, None]
    band_rows = 8

    def near_band(row_start):
        target = lax.dynamic_slice_in_dim(particles, row_start, band_rows, 2)
        real_sum = jnp.zeros((half_slots, band_rows, cells_x), jnp.float32)
        imag_sum = jnp.zeros((half_slots, band_rows, cells_x), jnp.float32)
        for step_y in (-1, 0, 1):
            row_band = lax.dynamic_slice_in_dim(framed, row_start + 1 + step_y, band_rows, 2)
            for step_x in (-1, 0, 1):
                source = row_band[:, :, :, 1 + step_x : 1 + step_x + cells_x]
                gap_x = target[0][:, None] - source[0][None] - step_x
                gap_y = target[1][:, None] - source[1][None] - step_y
                weight = source[2][None] / (gap_x * gap_x + gap_y * gap_y + blob_square)
                if step_x == 0 and step_y == 0:
                    weight = weight * keep_mask
                real_sum = real_sum + jnp.sum(weight * gap_x, axis=1)
                imag_sum = imag_sum - jnp.sum(weight * gap_y, axis=1)
        return jnp.stack([real_sum, imag_sum])

    starts = jnp.arange(0, cells_y, band_rows, dtype=jnp.int32)
    bands = lax.map(near_band, starts)
    near = bands.transpose(1, 2, 0, 3, 4).reshape(2, half_slots, cells_y, cells_x)
    real_part = near[0] + far_real
    imag_part = near[1] + far_imag
    return jnp.stack([imag_part, real_part]) / (2.0 * math.pi)


def solution(mesh):
    return jax.shard_map(
        local,
        mesh=mesh,
        in_specs=(
            P(None, "rep", "level", "cell"),
            P("rep", "level", "cell"),
            P(None, "rep", "level", "cell"),
            P("rep", "level", "cell"),
            P("rep", "level", "cell"),
            P("rep", "level", "cell"),
            P("rep", "level", "cell"),
        ),
        out_specs=P(None, "rep", "level", "cell"),
        check_vma=False,
    )
```

profile of v0, /device:TPU:10, one launch (start us, length us, event | category | flops | bytes accessed | tf_op | source)
XLA Modules:
  0.0 1255.9 jit_solution(15650942823292022477)
XLA Ops:
  14.8 16.1 %scatter_custom_fusion.1 = s32[16384]{0:T(1024)} fusion(s32[4096]{0:T(1024)S(1)} %broadcast_select_fusion.1, s32[4096]{0:T(1024)S(1)} %bitcast.975, s32[]{:T(128)} %constant.220.clone.1), kind=kCustom, calls=%fused_computation.410 | custom fusion | bytes 65540
  31.0 8.3 all-to-all-start
  42.2 14.7 %scatter_custom_fusion.2 = f32[3,16384]{0,1:T(8,128)} fusion(s32[4096]{0:T(1024)S(1)} %broadcast_select_fusion, f32[4096,3]{1,0:T(8,128)} %copy.2074, f32[]{:T(128)} %constant.218.clone.1), kind=kCustom, calls=%fused_computation.103 | custom fusion | bytes 197120
  56.9 5.9 copy.2075
  63.7 16.0 %copy.2076 = f32[3,65536]{0,1:T(8,128)} copy(f32[3,65536]{1,0:T(4,128)S(1)} %pad_maximum_fusion.1) | data formatting | bytes 1572864 | tf_op jit(solution)/shard_map/concatenate | solution.py:194
  80.2 7.2 all-to-all-start.1
  87.6 7.2 all-to-all-done.1
  99.8 62.4 %scatter_fusion = f32[3,65536]{0,1:T(8,128)} fusion(f32[3,65536]{0,1:T(8,128)} %copy.2076, s32[16384]{0:T(1024)S(1)} %bitcast.957, f32[16384,3]{1,0:T(8,128)} %copy.2077), kind=kCustom, calls=%fused_computation | custom fusion | bytes 655360 | tf_op jit(solution)/shard_map/scatter | solution.py:195
  162.2 20.2 %copy.2589 = f32[3,16,32,128]{3,2,1,0:T(8,128)} copy(f32[3,16,32,128]{0,3,2,1:T(8,128)} %bitcast.912) | data formatting | bytes 1572864 | tf_op jit(solution)/shard_map/reshape | solution.py:196
  182.5 35.0 %slice_reduce_fusion.1 = (f32[65536]{0:T(1024)}, f32[65536]{0:T(1024)}) fusion(f32[3,65536]{0,1:T(8,128)} %scatter_fusion), kind=kLoop, calls=%fused_computation.102 | loop fusion | bytes 1048576 | tf_op jit(solution)/shard_map/slice | solution.py:233
  247.6 177.4 %all-gather = f32[1280,2,8]{2,1,0:T(2,128)} all-gather(f32[20,2,8]{2,1,0:T(2,128)S(1)} %copy.2384), channel_id=2, replica_groups=mesh['cell'=16,'level'=4,'rep'=2] {'cell','level'}, dimensions={0}, use_global_device_ids=true | all-gather | bytes 83200 | tf_op jit(solution)/shard_map/all_gather | solution.py:207
  569.5 12.1 collective-permute-start.17
  625.3 6.7 collective-permute-start.19
  1042.2 9.6 concatenate.134
  1051.8 9.6 concatenate.135
  1061.4 9.6 concatenate.136
  1071.0 9.7 concatenate.137
  1080.7 5.7 convolution_bitcast_fusion.7
  1140.1 103.7 %while.16 = (s32[]{:T(128)}, f32[4,2,16,8,128]{4,3,2,1,0:T(8,128)}, s32[4]{0:T(128)}, f32[3,32,34,130]{3,2,1,0:T(8,128)}, f32[3,16,32,128]{3,2,1,0:T(8,128)}, /*...) while((s32[]{:T(128)}, f32[4,2,16,8,128]{4,3,2,1,0:T(8,128)}, ...), condition=%wide.region_25.26_spmd.clone, body=%wide.region_6.25_spmd.clone.sunk | while | flops 58737680 | bytes 14422976 | solution.py:260
  1145.8 7.4 dynamic-slice_bitcast_fusion.31
  1160.3 5.1 fusion.384
  1171.9 7.1 dynamic-slice_bitcast_fusion.31
  1197.7 7.3 dynamic-slice_bitcast_fusion.31
  1223.7 7.2 dynamic-slice_bitcast_fusion.31
  (1005 shorter events, 747.3 us)
Async XLA Ops:
  31.0 49.3 %all-to-all-start = ((s32[1,16,1024]{2,0,1:T(1,128)}), s32[1,16,1024]{2,0,1:T(1,128)S(1)}, u32[]{:S(2)}, u32[]{:S(2)}) async-start(s32[1,16,1024]{2,0,1:T(1,128)} %bitcast.8), calls=%async_computation | async-start | bytes 131072 | tf_op jit(solution)/shard_map/all_to_all | solution.py:192
  80.2 14.6 %all-to-all-start.1 = ((f32[3,16,1024]{2,0,1:T(4,128)}), f32[3,16,1024]{2,0,1:T(4,128)S(1)}, u32[]{:S(2)}, u32[]{:S(2)}) async-start(f32[3,16,1024]{2,0,1:T(4,128)} %copy.2075), calls=%async_computation.1 | async-start | bytes 524288 | tf_op jit(solution)/shard_map/all_to_all | solution.py:191
  87.5 130.0 %all-gather.3.cloned.1.call-start = ((), (), s32[]{:S(2)}) async-start(), calls=%async_computation.2 | async-start | bytes 2359296 | tf_op jit(solution)/shard_map/all_gather | solution.py:197
  235.6 396.5 %copy-start.9 = (f32[20,16,64]{2,0,1:T(8,128)}, f32[20,16,64]{2,0,1:T(8,128)S(1)}, u32[]{:S(2)}) copy-start(f32[20,16,64]{2,0,1:T(8,128)S(1)} %fusion.27) | copy-start | bytes 245764
  567.5 30.5 %collective-permute-start.16 = (f32[20,4,3]{0,2,1:T(4,128)S(1)}, f32[20,4,3]{0,2,1:T(4,128)S(1)}, u32[]{:S(2)}, u32[]{:S(2)}) collective-permute-start(f32[20,4,3]{0,2,1:T(4,128)S(1)} %get-tuple-element.364), channel_id=1, source_target_pairs={{0,8},{8,16},{16,24},{24,32},{32,40},{40,48},{48,56},{56,64},{64,7... | collective-permute-start | bytes 2888 | tf_op jit(solution)/shard_map/ppermute | solution.py:22
  569.5 32.6 %collective-permute-start.17 = (f32[20,4,3]{0,2,1:T(4,128)S(1)}, f32[20,4,3]{0,2,1:T(4,128)S(1)}, u32[]{:S(2)}, u32[]{:S(2)}) collective-permute-start(f32[20,4,3]{0,2,1:T(4,128)S(1)} %get-tuple-element.365), channel_id=1, source_target_pairs={{8,0},{16,8},{24,16},{32,24},{40,32},{48,40},{56,48},{64,56},{72,6... | collective-permute-start | bytes 2888 | tf_op jit(solution)/shard_map/ppermute | solution.py:23
  581.6 24.4 %collective-permute-start.12 = (f32[20,8,3]{2,0,1:T(8,128)S(1)}, f32[20,8,3]{2,0,1:T(8,128)S(1)}, u32[]{:S(2)}, u32[]{:S(2)}) collective-permute-start(f32[20,8,3]{2,0,1:T(8,128)S(1)} %get-tuple-element.360), channel_id=1, source_target_pairs={{0,8},{8,16},{16,24},{24,32},{32,40},{40,48},{48,56},{56,64},{64,7... | collective-permute-start | bytes 5768 | tf_op jit(solution)/shard_map/ppermute | solution.py:22
  583.5 26.5 %collective-permute-start.13 = (f32[20,8,3]{2,0,1:T(8,128)}, f32[20,8,3]{2,0,1:T(8,128)S(1)}, u32[]{:S(2)}, u32[]{:S(2)}) collective-permute-start(f32[20,8,3]{2,0,1:T(8,128)} %get-tuple-element.361), channel_id=1, source_target_pairs={{8,0},{16,8},{24,16},{32,24},{40,32},{48,40},{56,48},{64,56},{72,6... | collective-permute-start | bytes 5768 | tf_op jit(solution)/shard_map/ppermute | solution.py:23
  587.4 36.0 %collective-permute-start.8 = (f32[20,16,3]{2,0,1:T(8,128)}, f32[20,16,3]{2,0,1:T(8,128)S(1)}, u32[]{:S(2)}, u32[]{:S(2)}) collective-permute-start(f32[20,16,3]{2,0,1:T(8,128)} %get-tuple-element.356), channel_id=1, source_target_pairs={{0,8},{8,16},{16,24},{24,32},{32,40},{40,48},{48,56},{56,64},{64,7... | collective-permute-start | bytes 11528 | tf_op jit(solution)/shard_map/ppermute | solution.py:22
  598.1 27.2 %collective-permute-start.9 = (f32[20,16,3]{2,0,1:T(8,128)}, f32[20,16,3]{2,0,1:T(8,128)}, u32[]{:S(2)}, u32[]{:S(2)}) collective-permute-start(f32[20,16,3]{2,0,1:T(8,128)} %get-tuple-element.357), channel_id=1, source_target_pairs={{8,0},{16,8},{24,16},{32,24},{40,32},{48,40},{56,48},{64,56},{72,6... | collective-permute-start | bytes 11528 | tf_op jit(solution)/shard_map/ppermute | solution.py:23
  602.0 65.5 %collective-permute-start.4 = (f32[20,32,3]{2,1,0:T(8,128)}, f32[20,32,3]{2,1,0:T(8,128)S(1)}, u32[]{:S(2)}, u32[]{:S(2)}) collective-permute-start(f32[20,32,3]{2,1,0:T(8,128)} %get-tuple-element.352), channel_id=1, source_target_pairs={{0,8},{8,16},{16,24},{24,32},{32,40},{40,48},{48,56},{56,64},{64,7... | collective-permute-start | bytes 23048 | tf_op jit(solution)/shard_map/ppermute | solution.py:22
  606.0 66.0 %collective-permute-start.5 = (f32[20,32,3]{2,1,0:T(8,128)}, f32[20,32,3]{2,1,0:T(8,128)S(1)}, u32[]{:S(2)}, u32[]{:S(2)}) collective-permute-start(f32[20,32,3]{2,1,0:T(8,128)} %get-tuple-element.353), channel_id=1, source_target_pairs={{8,0},{16,8},{24,16},{32,24},{40,32},{48,40},{56,48},{64,56},{72,6... | collective-permute-start | bytes 23048 | tf_op jit(solution)/shard_map/ppermute | solution.py:23
  610.6 133.6 %collective-permute-start = (f32[3,32,32,1]{2,1,3,0:T(8,128)}, f32[3,32,32,1]{2,1,3,0:T(8,128)}, u32[]{:S(2)}, u32[]{:S(2)}) collective-permute-start(f32[3,32,32,1]{2,1,3,0:T(8,128)} %copy.2079), channel_id=1, source_target_pairs={{0,8},{8,16},{16,24},{24,32},{32,40},{40,48},{48,56},{56,64},{64,7... | collective-permute-start | bytes 36872 | tf_op jit(solution)/shard_map/ppermute | solution.py:22
  623.4 24.9 %collective-permute-start.18 = (f32[20,3,22]{0,2,1:T(8,128)}, f32[20,3,22]{0,2,1:T(8,128)}, u32[]{:S(2)}, u32[]{:S(2)}) collective-permute-start(f32[20,3,22]{0,2,1:T(8,128)} %get-tuple-element.362), channel_id=1, source_target_pairs={{0,2},{2,4},{4,6},{1,3},{3,5},{5,7},{8,10},{10,12},{12,14},{9,11},... | collective-permute-start | bytes 15848 | tf_op jit(solution)/shard_map/ppermute | solution.py:22
  625.3 27.4 %collective-permute-start.19 = (f32[20,3,22]{0,2,1:T(8,128)}, f32[20,3,22]{0,2,1:T(8,128)}, u32[]{:S(2)}, u32[]{:S(2)}) collective-permute-start(f32[20,3,22]{0,2,1:T(8,128)} %get-tuple-element.363), channel_id=1, source_target_pairs={{2,0},{4,2},{6,4},{3,1},{5,3},{7,5},{10,8},{12,10},{14,12},{11,9},... | collective-permute-start | bytes 15848 | tf_op jit(solution)/shard_map/ppermute | solution.py:23
  648.2 102.1 %collective-permute-start.1 = (f32[3,32,32,1]{2,1,3,0:T(8,128)}, f32[3,32,32,1]{2,1,3,0:T(8,128)}, u32[]{:S(2)}, u32[]{:S(2)}) collective-permute-start(f32[3,32,32,1]{2,1,3,0:T(8,128)} %copy.2080), channel_id=1, source_target_pairs={{8,0},{16,8},{24,16},{32,24},{40,32},{48,40},{56,48},{64,56},{72,6... | collective-permute-start | bytes 36872 | tf_op jit(solution)/shard_map/ppermute | solution.py:23
  652.8 42.0 %collective-permute-start.14 = (f32[20,3,38]{2,0,1:T(8,128)}, f32[20,3,38]{2,0,1:T(8,128)}, u32[]{:S(2)}, u32[]{:S(2)}) collective-permute-start(f32[20,3,38]{2,0,1:T(8,128)} %get-tuple-element.358), channel_id=1, source_target_pairs={{0,2},{2,4},{4,6},{1,3},{3,5},{5,7},{8,10},{10,12},{12,14},{9,11},... | collective-permute-start | bytes 27368 | tf_op jit(solution)/shard_map/ppermute | solution.py:22
  667.5 31.7 %collective-permute-start.15 = (f32[20,3,38]{2,0,1:T(8,128)}, f32[20,3,38]{2,0,1:T(8,128)S(1)}, u32[]{:S(2)}, u32[]{:S(2)}) collective-permute-start(f32[20,3,38]{2,0,1:T(8,128)} %get-tuple-element.359), channel_id=1, source_target_pairs={{2,0},{4,2},{6,4},{3,1},{5,3},{7,5},{10,8},{12,10},{14,12},{11,9},... | collective-permute-start | bytes 27368 | tf_op jit(solution)/shard_map/ppermute | solution.py:23
  672.8 85.2 %collective-permute-start.10 = (f32[20,3,70]{2,0,1:T(8,128)}, f32[20,3,70]{2,0,1:T(8,128)}, u32[]{:S(2)}, u32[]{:S(2)}) collective-permute-start(f32[20,3,70]{2,0,1:T(8,128)} %get-tuple-element.354), channel_id=1, source_target_pairs={{0,2},{2,4},{4,6},{1,3},{3,5},{5,7},{8,10},{10,12},{12,14},{9,11},... | collective-permute-start | bytes 50408 | tf_op jit(solution)/shard_map/ppermute | solution.py:22
  694.7 67.8 %collective-permute-start.11 = (f32[20,3,70]{2,0,1:T(8,128)}, f32[20,3,70]{2,0,1:T(8,128)}, u32[]{:S(2)}, u32[]{:S(2)}) collective-permute-start(f32[20,3,70]{2,0,1:T(8,128)} %get-tuple-element.355), channel_id=1, source_target_pairs={{2,0},{4,2},{6,4},{3,1},{5,3},{7,5},{10,8},{12,10},{14,12},{11,9},... | collective-permute-start | bytes 50408 | tf_op jit(solution)/shard_map/ppermute | solution.py:23
  699.3 201.4 %collective-permute-start.6 = (f32[20,3,134]{2,1,0:T(4,128)}, f32[20,3,134]{2,1,0:T(4,128)}, u32[]{:S(2)}, u32[]{:S(2)}) collective-permute-start(f32[20,3,134]{2,1,0:T(4,128)} %get-tuple-element.348), channel_id=1, source_target_pairs={{0,2},{2,4},{4,6},{1,3},{3,5},{5,7},{8,10},{10,12},{12,14},{9,11},... | collective-permute-start | bytes 96488 | tf_op jit(solution)/shard_map/ppermute | solution.py:22
  744.2 156.5 %collective-permute-start.7 = (f32[20,3,134]{2,1,0:T(4,128)}, f32[20,3,134]{2,1,0:T(4,128)}, u32[]{:S(2)}, u32[]{:S(2)}) collective-permute-start(f32[20,3,134]{2,1,0:T(4,128)} %get-tuple-element.349), channel_id=1, source_target_pairs={{2,0},{4,2},{6,4},{3,1},{5,3},{7,5},{10,8},{12,10},{14,12},{11,9},... | collective-permute-start | bytes 96488 | tf_op jit(solution)/shard_map/ppermute | solution.py:23
  755.5 377.6 %collective-permute-start.2 = (f32[3,32,1,130]{3,1,2,0:T(8,128)}, f32[3,32,1,130]{3,1,2,0:T(8,128)}, u32[]{:S(2)}, u32[]{:S(2)}) collective-permute-start(f32[3,32,1,130]{3,1,2,0:T(8,128)} %copy.2083), channel_id=1, source_target_pairs={{0,2},{2,4},{4,6},{1,3},{3,5},{5,7},{8,10},{10,12},{12,14},{9,11},... | collective-permute-start | bytes 149768 | tf_op jit(solution)/shard_map/ppermute | solution.py:22
  758.0 376.1 %collective-permute-start.3 = (f32[3,32,1,130]{3,1,2,0:T(8,128)}, f32[3,32,1,130]{3,1,2,0:T(8,128)}, u32[]{:S(2)}, u32[]{:S(2)}) collective-permute-start(f32[3,32,1,130]{3,1,2,0:T(8,128)} %copy.2084), channel_id=1, source_target_pairs={{2,0},{4,2},{6,4},{3,1},{5,3},{7,5},{10,8},{12,10},{14,12},{11,9},... | collective-permute-start | bytes 149768 | tf_op jit(solution)/shard_map/ppermute | solution.py:23
  (133 other events, 1695.6 us)
Sparse Core Ops, SparseCore 0:
  182.6 10.9 all-gather.2
where the time goes:
time: 1270 us; the launch traced here: 1260 us
  local copies, waits for them, and re-layouts  764 us (60%)
  blocking collectives  177 us (14%)
  matrix products  96.1 us (8%)
  starting transfers between devices  88.1 us (7%)
  other arithmetic  82.5 us (6%)
  loops' own time  23 us (2%)
  between operations  17.9 us (1%)
    slice x305, local copies, waits for them, and re-layouts, grouped_far(): padded[:, first_y:first_y + cells_y:2, first_x:first_x + cells_x:2]  335 us
    all_gather x1, blocking collectives, local(): lax.all_gather(coarse_own[None], ('cell', 'level'), axis=0, tiled=True)  177 us
    dot_general x96, matrix products, apply_matrix(): jnp.einsum('ij,jyx->iyx', jnp.asarray(matrix, dtype=jnp.float32), level_f...  89.4 us
    unnamed x315, local copies, waits for them, and re-layouts  80.3 us
    concatenate x28, local copies, waits for them, and re-layouts, grouped_far(): jnp.concatenate(pieces, axis=0)  77.2 us
    scatter x1, local copies, waits for them, and re-layouts, local(): resident.at[:, arrived_at.reshape(-1)]  62.4 us
    ppermute x10, starting transfers between devices, with_halo(): after = lax.ppermute(first, axis, down)  53.4 us
    reduce_sum x8, other arithmetic, near_band(): real_sum = real_sum + jnp.sum(weight * gap_x, axis=1)  36.7 us
  transfers between devices with their start and end apart: 23, of which 1 were waited for; matrix products, arithmetic and copies ran while one was open for 45% of the time, Pallas kernels for 0%

commit v1 on v0

--- a/solution.py
+++ b/solution.py
@@ -204,7 +204,15 @@
     framed_levels = [framing(owned[k]) for k in range(HALO_LEVELS)]
     coarse_own = owned[HALO_LEVELS]
     channels, coarse_y, coarse_x = coarse_own.shape
-    collected = lax.all_gather(coarse_own[None], ("cell", "level"), axis=0, tiled=True)
+    collected = jnp.concatenate(
+        lax.all_to_all(
+            jnp.stack([coarse_own[None]] * lax.axis_size(("cell", "level"))),
+            ("cell", "level"),
+            0,
+            0,
+        ),
+        axis=0,
+    )
     coarse_grid = collected.reshape(cell_count, level_count, channels, coarse_y, coarse_x)
     coarse_grid = coarse_grid.transpose(2, 1, 3, 0, 4).reshape(
         channels, level_count * coarse_y, cell_count * coarse_x

time: 1270 us -> 1020 us (0.80)
  the two profiles are of different devices: /device:TPU:10 before, /device:TPU:40 now
where the time goes in v1:
time: 1020 us; the launch traced here: 1010 us
  local copies, waits for them, and re-layouts  714 us (70%)
  starting transfers between devices  95.8 us (9%)
  other arithmetic  76 us (7%)
  matrix products  71.5 us (7%)
  loops' own time  24.4 us (2%)
  between operations  18 us (2%)
    slice x305, local copies, waits for them, and re-layouts, grouped_far(): padded[:, first_y:first_y + cells_y:2, first_x:first_x + cells_x:2]  315 us
    unnamed x320, local copies, waits for them, and re-layouts  82 us
    concatenate x28, local copies, waits for them, and re-layouts, grouped_far(): jnp.concatenate(pieces, axis=0)  70.2 us
    dot_general x96, matrix products, apply_matrix(): jnp.einsum('ij,jyx->iyx', jnp.asarray(matrix, dtype=jnp.float32), level_f...  66.8 us
    scatter x1, local copies, waits for them, and re-layouts, local(): resident.at[:, arrived_at.reshape(-1)]  62.4 us
    ppermute x10, starting transfers between devices, with_halo(): after = lax.ppermute(first, axis, down)  48.8 us
    reduce_sum x8, other arithmetic, near_band(): real_sum = real_sum + jnp.sum(weight * gap_x, axis=1)  36.7 us
    slice x1, local copies, waits for them, and re-layouts, local(): far_real, far_imag = evaluate(local_field, particles[0], particles[1])  35 us
  transfers between devices with their start and end apart: 24, of which 1 were waited for; matrix products, arithmetic and copies ran while one was open for 60% of the time, Pallas kernels for 0%

profile of v1, /device:TPU:40, one launch (start us, length us, event | category | flops | bytes accessed | tf_op | source)
XLA Modules:
  0.0 1006.6 jit_solution(7150480751780002980)
XLA Ops:
  14.8 16.1 %scatter_custom_fusion.1 = s32[16384]{0:T(1024)} fusion(s32[4096]{0:T(1024)S(1)} %broadcast_select_fusion.1, s32[4096]{0:T(1024)S(1)} %bitcast.978, s32[]{:T(128)} %constant.220.clone.1), kind=kCustom, calls=%fused_computation.410 | custom fusion | bytes 65540
  31.0 7.9 all-to-all-start
  40.4 14.4 %scatter_custom_fusion.2 = f32[3,16384]{0,1:T(8,128)} fusion(s32[4096]{0:T(1024)S(1)} %broadcast_select_fusion, f32[4096,3]{1,0:T(8,128)S(1)} %copy.2070, f32[]{:T(128)} %constant.218.clone.1), kind=kCustom, calls=%fused_computation.103 | custom fusion | bytes 196612
  54.8 5.9 copy.2071
  61.6 16.0 %copy.2072 = f32[3,65536]{0,1:T(8,128)} copy(f32[3,65536]{1,0:T(4,128)S(1)} %pad_maximum_fusion.1) | data formatting | bytes 1572864 | tf_op jit(solution)/shard_map/concatenate | solution.py:194
  77.6 7.2 all-to-all-start.1
  84.9 6.7 all-to-all-done.1
  96.6 62.4 %scatter_fusion = f32[3,65536]{0,1:T(8,128)} fusion(f32[3,65536]{0,1:T(8,128)} %copy.2072, s32[16384]{0:T(1024)S(1)} %bitcast.960, f32[16384,3]{1,0:T(8,128)} %copy.2073), kind=kCustom, calls=%fused_computation | custom fusion | bytes 655360 | tf_op jit(solution)/shard_map/scatter | solution.py:195
  159.0 20.2 %copy.2584 = f32[3,16,32,128]{3,2,1,0:T(8,128)} copy(f32[3,16,32,128]{0,3,2,1:T(8,128)} %bitcast.915) | data formatting | bytes 1572864 | tf_op jit(solution)/shard_map/reshape | solution.py:196
  179.2 35.0 %slice_reduce_fusion.1 = (f32[65536]{0:T(1024)}, f32[65536]{0:T(1024)}) fusion(f32[3,65536]{0,1:T(8,128)} %scatter_fusion), kind=kLoop, calls=%fused_computation.102 | loop fusion | bytes 1048576 | tf_op jit(solution)/shard_map/slice | solution.py:241
  247.7 8.6 all-to-all-start.2
  266.2 6.0 collective-permute-start.13
  281.7 6.0 collective-permute-start.9
  292.3 6.0 collective-permute-start.5
  332.7 6.0 collective-permute-start.1
  716.1 9.6 concatenate.134
  725.7 9.6 concatenate.135
  735.2 9.6 concatenate.136
  744.8 10.0 concatenate.137
  779.4 100.6 %while.16 = (s32[]{:T(128)}, f32[4,2,16,8,128]{4,3,2,1,0:T(8,128)}, s32[4]{0:T(128)}, f32[3,32,34,130]{3,2,1,0:T(8,128)}, f32[3,16,32,128]{3,2,1,0:T(8,128)}, /*...) while((s32[]{:T(128)}, f32[4,2,16,8,128]{4,3,2,1,0:T(8,128)}, ...), condition=%wide.region_25.26_spmd.clone, body=%wide.region_6.25_spmd.clone.sunk | while | flops 58737680 | bytes 13898660 | solution.py:268
  785.4 6.7 dynamic-slice_bitcast_fusion.31
  810.4 7.3 dynamic-slice_bitcast_fusion.31
  836.0 6.8 dynamic-slice_bitcast_fusion.31
  861.2 6.6 dynamic-slice_bitcast_fusion.31
  (1004 shorter events, 673.7 us)
Async XLA Ops:
  31.0 46.6 %all-to-all-start = ((s32[1,16,1024]{2,0,1:T(1,128)}), s32[1,16,1024]{2,0,1:T(1,128)S(1)}, u32[]{:S(2)}, u32[]{:S(2)}) async-start(s32[1,16,1024]{2,0,1:T(1,128)} %bitcast.8), calls=%async_computation | async-start | bytes 131072 | tf_op jit(solution)/shard_map/all_to_all | solution.py:192
  77.6 14.0 %all-to-all-start.1 = ((f32[3,16,1024]{2,0,1:T(4,128)}), f32[3,16,1024]{2,0,1:T(4,128)S(1)}, u32[]{:S(2)}, u32[]{:S(2)}) async-start(f32[3,16,1024]{2,0,1:T(4,128)} %copy.2071), calls=%async_computation.1 | async-start | bytes 524288 | tf_op jit(solution)/shard_map/all_to_all | solution.py:191
  84.8 129.4 %all-gather.2.cloned.1.call-start = ((), (), s32[]{:S(2)}) async-start(), calls=%async_computation.3 | async-start | bytes 2359296 | tf_op jit(solution)/shard_map/all_gather | solution.py:197
  247.7 634.2 %all-to-all-start.2 = ((f32[64,1,320]{2,1,0:T(1,128)}), f32[64,1,320]{2,1,0:T(1,128)}, u32[]{:S(2)}, u32[]{:S(2)}) async-start(f32[64,1,320]{2,1,0:T(1,128)} %reshape.1376), calls=%async_computation.2 | async-start | bytes 196608 | tf_op jit(solution)/shard_map/all_to_all | solution.py:208
  256.3 25.4 %collective-permute-start.16 = (f32[20,4,3]{0,2,1:T(4,128)S(1)}, f32[20,4,3]{0,2,1:T(4,128)S(1)}, u32[]{:S(2)}, u32[]{:S(2)}) collective-permute-start(f32[20,4,3]{0,2,1:T(4,128)S(1)} %get-tuple-element.364), channel_id=1, source_target_pairs={{0,8},{8,16},{16,24},{24,32},{32,40},{40,48},{48,56},{56,64},{64,7... | collective-permute-start | bytes 2888 | tf_op jit(solution)/shard_map/ppermute | solution.py:22
  259.7 28.1 %collective-permute-start.17 = (f32[20,4,3]{0,2,1:T(4,128)S(1)}, f32[20,4,3]{0,2,1:T(4,128)S(1)}, u32[]{:S(2)}, u32[]{:S(2)}) collective-permute-start(f32[20,4,3]{0,2,1:T(4,128)S(1)} %get-tuple-element.365), channel_id=1, source_target_pairs={{8,0},{16,8},{24,16},{32,24},{40,32},{48,40},{56,48},{64,56},{72,6... | collective-permute-start | bytes 2888 | tf_op jit(solution)/shard_map/ppermute | solution.py:23
  264.3 28.0 %collective-permute-start.12 = (f32[20,8,3]{2,0,1:T(8,128)}, f32[20,8,3]{2,0,1:T(8,128)S(1)}, u32[]{:S(2)}, u32[]{:S(2)}) collective-permute-start(f32[20,8,3]{2,0,1:T(8,128)} %get-tuple-element.360), channel_id=1, source_target_pairs={{0,8},{8,16},{16,24},{24,32},{32,40},{40,48},{48,56},{56,64},{64,7... | collective-permute-start | bytes 5768 | tf_op jit(solution)/shard_map/ppermute | solution.py:22
  266.2 32.1 %collective-permute-start.13 = (f32[20,8,3]{2,0,1:T(8,128)}, f32[20,8,3]{2,0,1:T(8,128)S(1)}, u32[]{:S(2)}, u32[]{:S(2)}) collective-permute-start(f32[20,8,3]{2,0,1:T(8,128)} %get-tuple-element.361), channel_id=1, source_target_pairs={{8,0},{16,8},{24,16},{32,24},{40,32},{48,40},{56,48},{64,56},{72,6... | collective-permute-start | bytes 5768 | tf_op jit(solution)/shard_map/ppermute | solution.py:23
  272.2 38.0 %collective-permute-start.8 = (f32[20,16,3]{2,0,1:T(8,128)}, f32[20,16,3]{2,0,1:T(8,128)S(1)}, u32[]{:S(2)}, u32[]{:S(2)}) collective-permute-start(f32[20,16,3]{2,0,1:T(8,128)} %get-tuple-element.356), channel_id=1, source_target_pairs={{0,8},{8,16},{16,24},{24,32},{32,40},{40,48},{48,56},{56,64},{64,7... | collective-permute-start | bytes 11528 | tf_op jit(solution)/shard_map/ppermute | solution.py:22
  281.7 31.8 %collective-permute-start.9 = (f32[20,16,3]{2,0,1:T(8,128)}, f32[20,16,3]{2,0,1:T(8,128)}, u32[]{:S(2)}, u32[]{:S(2)}) collective-permute-start(f32[20,16,3]{2,0,1:T(8,128)} %get-tuple-element.357), channel_id=1, source_target_pairs={{8,0},{16,8},{24,16},{32,24},{40,32},{48,40},{56,48},{64,56},{72,6... | collective-permute-start | bytes 11528 | tf_op jit(solution)/shard_map/ppermute | solution.py:23
  287.8 64.0 %collective-permute-start.4 = (f32[20,32,3]{2,1,0:T(8,128)}, f32[20,32,3]{2,1,0:T(8,128)S(1)}, u32[]{:S(2)}, u32[]{:S(2)}) collective-permute-start(f32[20,32,3]{2,1,0:T(8,128)} %get-tuple-element.352), channel_id=1, source_target_pairs={{0,8},{8,16},{16,24},{24,32},{32,40},{40,48},{48,56},{56,64},{64,7... | collective-permute-start | bytes 23048 | tf_op jit(solution)/shard_map/ppermute | solution.py:22
  292.3 63.1 %collective-permute-start.5 = (f32[20,32,3]{2,1,0:T(8,128)}, f32[20,32,3]{2,1,0:T(8,128)S(1)}, u32[]{:S(2)}, u32[]{:S(2)}) collective-permute-start(f32[20,32,3]{2,1,0:T(8,128)} %get-tuple-element.353), channel_id=1, source_target_pairs={{8,0},{16,8},{24,16},{32,24},{40,32},{48,40},{56,48},{64,56},{72,6... | collective-permute-start | bytes 23048 | tf_op jit(solution)/shard_map/ppermute | solution.py:23
  298.3 126.1 %collective-permute-start = (f32[3,32,32,1]{2,1,3,0:T(8,128)}, f32[3,32,32,1]{2,1,3,0:T(8,128)}, u32[]{:S(2)}, u32[]{:S(2)}) collective-permute-start(f32[3,32,32,1]{2,1,3,0:T(8,128)} %copy.2075), channel_id=1, source_target_pairs={{0,8},{8,16},{16,24},{24,32},{32,40},{40,48},{48,56},{56,64},{64,7... | collective-permute-start | bytes 36872 | tf_op jit(solution)/shard_map/ppermute | solution.py:22
  310.2 22.5 %collective-permute-start.18 = (f32[20,3,22]{0,2,1:T(8,128)}, f32[20,3,22]{0,2,1:T(8,128)}, u32[]{:S(2)}, u32[]{:S(2)}) collective-permute-start(f32[20,3,22]{0,2,1:T(8,128)} %get-tuple-element.362), channel_id=1, source_target_pairs={{0,2},{2,4},{4,6},{1,3},{3,5},{5,7},{8,10},{10,12},{12,14},{9,11},... | collective-permute-start | bytes 15848 | tf_op jit(solution)/shard_map/ppermute | solution.py:22
  313.6 25.2 %collective-permute-start.19 = (f32[20,3,22]{0,2,1:T(8,128)}, f32[20,3,22]{0,2,1:T(8,128)}, u32[]{:S(2)}, u32[]{:S(2)}) collective-permute-start(f32[20,3,22]{0,2,1:T(8,128)} %get-tuple-element.363), channel_id=1, source_target_pairs={{2,0},{4,2},{6,4},{3,1},{5,3},{7,5},{10,8},{12,10},{14,12},{11,9},... | collective-permute-start | bytes 15848 | tf_op jit(solution)/shard_map/ppermute | solution.py:23
  332.7 97.7 %collective-permute-start.1 = (f32[3,32,32,1]{2,1,3,0:T(8,128)}, f32[3,32,32,1]{2,1,3,0:T(8,128)}, u32[]{:S(2)}, u32[]{:S(2)}) collective-permute-start(f32[3,32,32,1]{2,1,3,0:T(8,128)} %copy.2076), channel_id=1, source_target_pairs={{8,0},{16,8},{24,16},{32,24},{40,32},{48,40},{56,48},{64,56},{72,6... | collective-permute-start | bytes 36872 | tf_op jit(solution)/shard_map/ppermute | solution.py:23
  338.7 41.1 %collective-permute-start.14 = (f32[20,3,38]{2,0,1:T(8,128)}, f32[20,3,38]{2,0,1:T(8,128)}, u32[]{:S(2)}, u32[]{:S(2)}) collective-permute-start(f32[20,3,38]{2,0,1:T(8,128)} %get-tuple-element.358), channel_id=1, source_target_pairs={{0,2},{2,4},{4,6},{1,3},{3,5},{5,7},{8,10},{10,12},{12,14},{9,11},... | collective-permute-start | bytes 27368 | tf_op jit(solution)/shard_map/ppermute | solution.py:22
  351.7 32.3 %collective-permute-start.15 = (f32[20,3,38]{2,0,1:T(8,128)}, f32[20,3,38]{2,0,1:T(8,128)S(1)}, u32[]{:S(2)}, u32[]{:S(2)}) collective-permute-start(f32[20,3,38]{2,0,1:T(8,128)} %get-tuple-element.359), channel_id=1, source_target_pairs={{2,0},{4,2},{6,4},{3,1},{5,3},{7,5},{10,8},{12,10},{14,12},{11,9},... | collective-permute-start | bytes 27368 | tf_op jit(solution)/shard_map/ppermute | solution.py:23
  356.1 82.0 %collective-permute-start.10 = (f32[20,3,70]{2,0,1:T(8,128)}, f32[20,3,70]{2,0,1:T(8,128)}, u32[]{:S(2)}, u32[]{:S(2)}) collective-permute-start(f32[20,3,70]{2,0,1:T(8,128)} %get-tuple-element.354), channel_id=1, source_target_pairs={{0,2},{2,4},{4,6},{1,3},{3,5},{5,7},{8,10},{10,12},{12,14},{9,11},... | collective-permute-start | bytes 50408 | tf_op jit(solution)/shard_map/ppermute | solution.py:22
  379.8 63.1 %collective-permute-start.11 = (f32[20,3,70]{2,0,1:T(8,128)}, f32[20,3,70]{2,0,1:T(8,128)}, u32[]{:S(2)}, u32[]{:S(2)}) collective-permute-start(f32[20,3,70]{2,0,1:T(8,128)} %get-tuple-element.355), channel_id=1, source_target_pairs={{2,0},{4,2},{6,4},{3,1},{5,3},{7,5},{10,8},{12,10},{14,12},{11,9},... | collective-permute-start | bytes 50408 | tf_op jit(solution)/shard_map/ppermute | solution.py:23
  384.0 190.5 %collective-permute-start.6 = (f32[20,3,134]{2,1,0:T(4,128)}, f32[20,3,134]{2,1,0:T(4,128)}, u32[]{:S(2)}, u32[]{:S(2)}) collective-permute-start(f32[20,3,134]{2,1,0:T(4,128)} %get-tuple-element.348), channel_id=1, source_target_pairs={{0,2},{2,4},{4,6},{1,3},{3,5},{5,7},{8,10},{10,12},{12,14},{9,11},... | collective-permute-start | bytes 96488 | tf_op jit(solution)/shard_map/ppermute | solution.py:22
  424.4 150.2 %collective-permute-start.7 = (f32[20,3,134]{2,1,0:T(4,128)}, f32[20,3,134]{2,1,0:T(4,128)}, u32[]{:S(2)}, u32[]{:S(2)}) collective-permute-start(f32[20,3,134]{2,1,0:T(4,128)} %get-tuple-element.349), channel_id=1, source_target_pairs={{2,0},{4,2},{6,4},{3,1},{5,3},{7,5},{10,8},{12,10},{14,12},{11,9},... | collective-permute-start | bytes 96488 | tf_op jit(solution)/shard_map/ppermute | solution.py:23
  435.6 338.1 %collective-permute-start.2 = (f32[3,32,1,130]{3,1,2,0:T(8,128)}, f32[3,32,1,130]{3,1,2,0:T(8,128)}, u32[]{:S(2)}, u32[]{:S(2)}) collective-permute-start(f32[3,32,1,130]{3,1,2,0:T(8,128)} %copy.2079), channel_id=1, source_target_pairs={{0,2},{2,4},{4,6},{1,3},{3,5},{5,7},{8,10},{10,12},{12,14},{9,11},... | collective-permute-start | bytes 149768 | tf_op jit(solution)/shard_map/ppermute | solution.py:22
  438.1 336.5 %collective-permute-start.3 = (f32[3,32,1,130]{3,1,2,0:T(8,128)}, f32[3,32,1,130]{3,1,2,0:T(8,128)}, u32[]{:S(2)}, u32[]{:S(2)}) collective-permute-start(f32[3,32,1,130]{3,1,2,0:T(8,128)} %copy.2080), channel_id=1, source_target_pairs={{2,0},{4,2},{6,4},{3,1},{5,3},{7,5},{10,8},{12,10},{14,12},{11,9},... | collective-permute-start | bytes 149768 | tf_op jit(solution)/shard_map/ppermute | solution.py:23
  (131 other events, 1474.8 us)
Sparse Core Ops, SparseCore 0:
  179.4 11.5 all-gather.1
